TPU v7x, 256 devices: a whole 4x4x8 slice. The times are simulated.
256 devices in a mesh: ctx: 32 (over y, x, z_lo), exp: 8 (over z_hi, core).
Axes of the slice: x: 4, y: 4, z: 8 (z_hi: 4, z_lo: 2; z = z_hi * 2 + z_lo), core: 2. Of those that a mesh axis runs over, the one named last changes fastest.
Arguments:
- queries: bfloat16 [4096, 32, 576], P('ctx', 'exp'), may hold values from -32 to 32
- key_latents: bfloat16 [2048, 576], P('ctx'), may hold values from -8 to 8
- query_pos: int32 [4096], P('ctx'), may hold values from 1 to 2047
- value_up: bfloat16 [32, 512, 128], P('exp'), may hold values from -0.25 to 0.25
- out_proj: bfloat16 [32, 128, 2304], P('exp'), may hold values from -0.09375 to 0.09375
- stream: bfloat16 [4096, 2304], P('ctx'), may hold values from -6 to 6
- norm_gain: bfloat16 [2304], replicated, may hold values from 0.099609375 to 1.8984375
- expert_ids: int32 [4096, 8], P('ctx'), may hold values from 0 to 255, all different within a row; in each aligned block of 128 rows (0 to 127, 128 to 255, ...) at most 8 rows name the same one
- gate_weights: float32 [4096, 8], P('ctx'), may hold values from 0.05 to 0.4
- w_gate: bfloat16 [256, 2304, 512], P(('ctx', 'exp')), may hold values from -0.125 to 0.125
- w_up: bfloat16 [256, 2304, 512], P(('ctx', 'exp')), may hold values from -0.125 to 0.125
- w_down: bfloat16 [256, 512, 2304], P(('ctx', 'exp')), may hold values from -0.25 to 0.25
- out_grad: bfloat16 [4096, 2304], P('ctx'), may hold values from -6 to 6
Outputs:
- stream_grad: bfloat16 [4096, 2304], P('ctx')
- query_grad: bfloat16 [4096, 32, 576], P('ctx', 'exp')
- key_grad: bfloat16 [2048, 576], P('ctx')
Inputs may be any that keep to these rules, and one draw needn't show every extreme that they name: `expert_ids`: in the rows of one index of ctx no expert is named by more than 8 rows, a bound that some block reaches; a row names 8 different experts. Row r sees context tokens 0 to query_pos[r].
All inputs are finite; a program needn't handle non-finite values.
Results may differ from a plain program's by a relative error of at most 0.015.
Values may be sent and summed in bfloat16 or wider, within the bound.
No kernel may reach another device: no remote copies, remote signals or barrier semaphores. Data moves between devices by JAX's collectives and lax.ppermute only.
A program may use at most 128 MiB of HBM per device.

v0:
```python
import functools

import jax
import jax.numpy as jnp
from jax import lax
from jax.experimental import pallas as pl
from jax.experimental.pallas import tpu as pltpu
from jax.sharding import Mesh, PartitionSpec as P

LAT = 512
ROPE = 64
VHEAD = 128
PACK = 4
SLOTS = 8
TOP = 8
EPSILON = 1e-06
SCALE = (VHEAD + ROPE) ** (-0.5)
BF = jnp.bfloat16
F32 = jnp.float32
CTX = ("y", "x", "zl")
EXP = ("zh", "co")
MIB = 1 << 20


def dot(left, right):
    return jnp.dot(left, right, preferred_element_type=F32)


def contract_last(left, right):
    return lax.dot_general(left, right, (((1,), (1,)), ((), ())), preferred_element_type=F32)


def contract_first(left, right):
    return lax.dot_general(left, right, (((0,), (0,)), ((), ())), preferred_element_type=F32)


def call(body, outs, args, vmem_mib, flops=0, scratch=(), far=(), far_out=()):
    size = sum(a.size * a.dtype.itemsize for a in args) + sum(
        o.size * jnp.dtype(o.dtype).itemsize for o in outs
    )

    def place(away):
        return pl.BlockSpec(memory_space=pltpu.HBM if away else pltpu.VMEM)

    return pl.pallas_call(
        body,
        out_shape=tuple(outs),
        in_specs=[place(i in far) for i in range(len(args))],
        out_specs=tuple(place(i in far_out) for i in range(len(outs))),
        scratch_shapes=list(scratch),
        compiler_params=pltpu.CompilerParams(vmem_limit_bytes=vmem_mib * MIB),
        cost_estimate=pl.CostEstimate(flops=flops, bytes_accessed=size, transcendentals=0),
    )(*args)


def shape(dims, dtype):
    return jax.ShapeDtypeStruct(dims, dtype)


def position():
    core, group = lax.axis_index("co"), lax.axis_index("zh")
    return group * 2 + core, core, group


def spread(row_ref):
    rows = row_ref[...].astype(F32)
    return jnp.concatenate([rows[i : i + 1, :] for i in range(rows.shape[0])], axis=1)


def prep_kernel(exp_count, *refs):
    pos = position()
    far, (send_far, weight), held, arrived = refs[:6], refs[6:8], refs[8:14], refs[14]
    send, left = refs[15], refs[16]
    stores = []

    def leave(at, wide):
        lanes = pl.ds(at, wide)
        store = pltpu.make_async_copy(
            send.at[:, lanes], send_far.at[:, lanes], left.at[len(stores)]
        )
        store.start()
        stores.append(store)

    copies = [
        pltpu.make_async_copy(source, target, arrived.at[i])
        for i, (source, target) in enumerate(zip(far, held))
    ]
    for copy in copies:
        copy.start()
    ids, gates, stream, gain, out_grad, keys = held
    copies[0].wait()
    copies[1].wait()
    rows, width = stream.shape
    slots = weight.shape[0]
    place = lax.broadcasted_iota(jnp.int32, (slots, rows), 0)
    expert = (place // SLOTS) * exp_count + pos[0]
    member = jnp.zeros((slots, rows), F32)
    weighting = jnp.zeros((slots, rows), F32)
    for k in range(ids.shape[0]):
        hit = ids[k : k + 1, :] == expert
        member = jnp.where(hit, 1.0, member)
        weighting = jnp.where(hit, gates[k : k + 1, :], weighting)
    before = (
        lax.broadcasted_iota(jnp.int32, (rows, rows), 0)
        < lax.broadcasted_iota(jnp.int32, (rows, rows), 1)
    ).astype(F32).astype(BF)
    rank = dot(member.astype(BF), before)
    chosen = (member > 0.5) & (rank == (place % SLOTS).astype(F32))
    select = jnp.where(chosen, 1.0, 0.0).astype(BF)
    weight[...] = jnp.where(chosen, weighting, 0.0)
    step = width // 3
    copies[4].wait()
    for c in range(0, width, step):
        send[:, width + c : width + c + step] = dot(select, out_grad[:, c : c + step]).astype(BF)
        leave(width + c, step)
    copies[5].wait()
    count = keys.shape[0]
    row = lax.broadcasted_iota(jnp.int32, (SLOTS, count), 0)
    key = lax.broadcasted_iota(jnp.int32, (SLOTS, count), 1)
    parts, ropes = [], []
    for q in range(PACK):
        wanted = pos[1] * (count // 2) + q * SLOTS + row
        pick = jnp.where(key == wanted, 1.0, 0.0).astype(BF)
        parts.append(dot(pick, keys[:, :LAT]))
        ropes.append(dot(pick, keys[:, LAT:]))
    parts.append(jnp.concatenate(ropes, axis=1))
    at = 2 * width
    for part in parts:
        wide = part.shape[1]
        part = jnp.broadcast_to(part[None], (slots // SLOTS, SLOTS, wide))
        send[:, at : at + wide] = part.reshape(slots, wide).astype(BF)
        leave(at, wide)
        at += wide
    copies[2].wait()
    copies[3].wait()
    stream_f = stream[...].astype(F32)
    inv_rms = lax.rsqrt(jnp.mean(stream_f * stream_f, axis=1, keepdims=True) + EPSILON)
    normed = (stream_f * inv_rms * spread(gain)).astype(BF)
    for c in range(0, width, step):
        send[:, c : c + step] = dot(select, normed[:, c : c + step]).astype(BF)
        leave(c, step)
    for store in stores:
        store.wait()


def expert_kernel(rows, w_gate, w_up, w_down, grads_far, key_pack, grads, arrived):
    width = w_gate.shape[0]
    stores = [pltpu.make_async_copy(rows.at[:, 2 * width :], key_pack, arrived.at[0])]
    stores[0].start()
    act_gate = dot(rows[:, :width], w_gate[...])
    act_up = dot(rows[:, :width], w_up[...])
    hidden_back = contract_last(rows[:, width : 2 * width], w_down[...])
    sig = jax.nn.sigmoid(act_gate)
    gate_back = (hidden_back * act_up * sig * (1.0 + act_gate * (1.0 - sig))).astype(BF)
    up_back = (hidden_back * act_gate * sig).astype(BF)
    step = width // 3
    for c in range(0, width, step):
        grads[:, c : c + step] = (
            contract_last(gate_back, w_gate[c : c + step, :])
            + contract_last(up_back, w_up[c : c + step, :])
        ).astype(BF)
        lanes = pl.ds(c, step)
        stores.append(
            pltpu.make_async_copy(
                grads.at[:, lanes], grads_far.at[:, lanes], arrived.at[len(stores)]
            )
        )
        stores[-1].start()
    for store in stores:
        store.wait()


def order_kernel(weight, ordered):
    pos = position()
    w = weight[...]
    high = w.astype(BF)
    low = (w - high.astype(F32)).astype(BF)
    rows = w.shape[1]
    piece = rows // 8
    core, chip = pos[1], pos[2]
    place = lax.broadcasted_iota(jnp.int32, (1, rows), 1)
    part, within = (place // piece) % 4, place % piece
    side = jnp.where(place < rows // 2, core, 1 - core)
    at_chip = jnp.where(part == 0, chip, jnp.where(part == 1, chip + 3, chip + 2 - side)) % 4
    half = jnp.where(part < 2, side, part - 2)
    source = (at_chip * 2 + half) * piece + within
    index = lax.broadcasted_iota(jnp.int32, (rows, rows), 0)
    moved = jnp.where(index == source, 1.0, 0.0).astype(BF)
    slots = w.shape[0]
    for i, source in enumerate((high, low)):
        turned = lax.dot_general(
            moved, source, (((0,), (1,)), ((), ())), preferred_element_type=F32
        )
        ordered[:, i * slots : (i + 1) * slots] = turned.astype(BF)


def combine_kernel(part, returned, ordered, out):
    half, width = out.shape
    slots = returned.shape[0]
    rows = slice(part * half, (part + 1) * half)
    step = width // 3
    for c in range(0, width, step):
        block = returned[:, c : c + step]
        total = dot(ordered[rows, :slots], block) + dot(ordered[rows, slots:], block)
        out[:, c : c + step] = total.astype(out.dtype)


def pair_kernel(keep, received, own, near, far):
    total = (keep[...] + received[...].astype(F32)).astype(BF)
    piece = own.shape[0]
    own[...] = total[:piece, :]
    near[...] = total[piece : 2 * piece, :]
    far[...] = total[2 * piece :, :]


def stream_kernel(
    own, own_2, far, far_2, near, near_2, stream, gain, out_grad, stream_grad, half_grad
):
    pos = position()
    first = pos[1] == 0
    piece, width = own.shape
    rows = 2 * piece

    def ordered(mine, other):
        a, b = mine[...].astype(F32), other[...].astype(F32)
        return jnp.where(first, a, b), jnp.where(first, b, a)

    below, above = ordered(far, far_2)
    normed_grad = jnp.concatenate(ordered(own, own_2), axis=0) + below + above
    normed_grad = normed_grad + jnp.concatenate(ordered(near, near_2), axis=0)
    here = pl.ds(pl.multiple_of(pos[2] * rows, rows), rows)
    stream_f = stream[here, :].astype(F32)
    gain_f = spread(gain)
    inv_rms = lax.rsqrt(jnp.mean(stream_f * stream_f, axis=1, keepdims=True) + EPSILON)
    scaled = normed_grad * gain_f
    branch = inv_rms * scaled - stream_f * (inv_rms * inv_rms * inv_rms) * jnp.mean(
        scaled * stream_f, axis=1, keepdims=True
    )
    result = (out_grad[here, :].astype(F32) + branch).astype(BF)
    stream_grad[...] = result
    half_grad[...] = jnp.where(first, result[:piece, :], result[piece:, :])


def latent_kernel(
    own,
    far,
    far_2,
    near,
    near_2,
    out_proj,
    value_up,
    latent_out,
    stream_far,
    latent_t,
    latent_rows,
    delta,
    stream_grad,
    sent,
):
    _, core, chip = position()
    piece = near.shape[0]

    def put(value, place, side):
        at = pl.multiple_of((lax.rem(chip + place, 4) * 2 + side) * piece, piece)
        stream_grad[pl.ds(at, value.shape[0]), :] = value[...]

    put(own, 0, 0)
    put(far, 2 + core, 0)
    put(far_2, 3 - core, 0)
    put(near, 1, core)
    put(near_2, 1, 1 - core)
    store = pltpu.make_async_copy(stream_grad, stream_far, sent.at[0])
    store.start()
    heads, lat, vhead = value_up.shape
    count = stream_grad.shape[0]
    all_rows = stream_grad[...]
    for h in range(heads):
        head_t = contract_last(out_proj[h], all_rows).astype(BF)
        grad_t = dot(value_up[h], head_t).astype(BF)
        cols = slice(h * count, (h + 1) * count)
        latent_t[:, cols] = grad_t
        grad_f = grad_t.astype(F32)
        delta[:, cols] = jnp.sum(grad_f * latent_out[:, cols], axis=0, keepdims=True)
        latent_rows[cols, :] = grad_f.T.astype(BF)
    store.wait()


def rope_lanes(q):
    at = PACK * LAT + (q // 2) * 2 * ROPE
    return slice(at, at + 2 * ROPE)


def scores_kernel(
    mine_far,
    other_far,
    queries_t,
    seen,
    probs_far,
    latent_far,
    rows_far,
    mine,
    other,
    scratch,
    probs,
    latent_out,
    query_rows,
    arrived,
):
    pos = position()
    heads, width, rows = queries_t.shape
    slots = mine.shape[0]
    count = heads * rows
    loads = [
        pltpu.make_async_copy(mine_far, mine, arrived.at[0]),
        pltpu.make_async_copy(other_far, other, arrived.at[1]),
    ]
    for load in loads:
        load.start()
    blank = jnp.zeros((ROPE, count), BF)
    query = jnp.concatenate([queries_t[h] for h in range(heads)], axis=1)
    rope = query[LAT:, :]
    ropes = [jnp.concatenate([rope, blank], axis=0), jnp.concatenate([blank, rope], axis=0)]
    stacked = jnp.concatenate([query[:LAT, :]] + ropes, axis=0)
    query_rows[...] = stacked.astype(F32).T.astype(BF)
    stores = [pltpu.make_async_copy(query_rows, rows_far, arrived.at[2])]
    stores[0].start()
    last = jnp.concatenate([seen[...]] * heads, axis=1)
    place = lax.broadcasted_iota(jnp.int32, (slots, 1), 0)
    slot_key = (place // SLOTS) * (2 * PACK * SLOTS) + place % SLOTS
    top = jnp.full((1, count), -jnp.inf, F32)
    for side, keys in enumerate((mine, other)):
        loads[side].wait()
        core = pos[1] if side == 0 else 1 - pos[1]
        for q in range(PACK):
            s = dot(keys[:, q * LAT : (q + 1) * LAT], query[:LAT, :])
            s = (s + dot(keys[:, rope_lanes(q)], ropes[q % 2])) * SCALE
            key = slot_key + (core * (PACK * SLOTS) + q * SLOTS)
            s = jnp.where(key <= last, s, -jnp.inf)
            scratch[side * PACK + q] = s
            top = jnp.maximum(top, jnp.max(s, axis=0, keepdims=True))
    total = jnp.zeros((1, count), F32)
    for c in range(2 * PACK):
        e = jnp.exp(scratch[c] - top)
        scratch[c] = e
        total = total + jnp.sum(e, axis=0, keepdims=True)
    inverse = 1.0 / total
    for c in range(2 * PACK):
        q = c % PACK
        p = (scratch[c] * inverse).astype(BF)
        probs[c] = p
        store = pltpu.make_async_copy(probs.at[c], probs_far.at[c], arrived.at[3 + c])
        store.start()
        stores.append(store)
        part = contract_first((mine if c < PACK else other)[:, q * LAT : (q + 1) * LAT], p)
        if c == 0:
            latent_out[...] = part
        else:
            latent_out[...] += part
    store = pltpu.make_async_copy(latent_out, latent_far, arrived.at[3 + 2 * PACK])
    store.start()
    for store in stores + [store]:
        store.wait()


def score_gradient(keys, p, q, latent_t, delta):
    prob_grad = dot(keys[:, q * LAT : (q + 1) * LAT], latent_t)
    return (p.astype(F32) * (prob_grad - delta) * SCALE).astype(BF)


def back_kernel(side, keys, probs, latent_t, latent_rows, delta, query_rows, key_grad):
    part = []
    for q in range(PACK):
        p = probs[side * PACK + q]
        sg = score_gradient(keys, p, q, latent_t[...], delta[...])
        key_grad[:, q * LAT : (q + 1) * LAT] = (
            dot(sg, query_rows[:, :LAT]) + dot(p, latent_rows[...])
        ).astype(BF)
        at = LAT + (q % 2) * 2 * ROPE
        part.append(dot(sg, query_rows[:, at : at + 2 * ROPE]))
        if q % 2:
            key_grad[:, rope_lanes(q)] = (part[q - 1] + part[q]).astype(BF)


def query_kernel(mine, other, probs, latent_t, delta, out):
    heads, width, rows = out.shape
    for pair in range(heads // 2):
        cols = slice(2 * pair * rows, 2 * (pair + 1) * rows)
        total = rope = None
        for side, keys in enumerate((mine, other)):
            for q in range(PACK):
                p = probs[side * PACK + q, :, cols]
                sg = score_gradient(keys, p, q, latent_t[:, cols], delta[:, cols])
                lat_part = contract_first(keys[:, q * LAT : (q + 1) * LAT], sg)
                rope_part = contract_first(keys[:, rope_lanes(q)], sg)
                rope_part = rope_part[(q % 2) * ROPE : (q % 2 + 1) * ROPE, :]
                total = lat_part if total is None else total + lat_part
                rope = rope_part if rope is None else rope + rope_part
        for i in range(2):
            own = slice(i * rows, (i + 1) * rows)
            out[2 * pair + i] = jnp.concatenate([total[:, own], rope[:, own]], axis=0).astype(BF)


def add_kernel(left, right, out_far, out, sent):
    stores = []
    piece = out.shape[0] // 4
    for i in range(4):
        here = pl.ds(i * piece, piece)
        out[here, :] = (left[here, :].astype(F32) + right[here, :].astype(F32)).astype(BF)
        stores.append(pltpu.make_async_copy(out.at[here, :], out_far.at[here, :], sent.at[i]))
        stores[-1].start()
    for store in stores:
        store.wait()


def sum_kernel(parts, out):
    count, width = parts.shape
    spread = parts[...].astype(F32).reshape(count // SLOTS, SLOTS, width)
    out[...] = jnp.sum(spread, axis=0).astype(BF)


def join_kernel(own, near, out):
    pos = position()
    first = pos[1] == 0
    a, b = own[...].astype(F32), near[...].astype(F32)
    out[...] = jnp.concatenate([jnp.where(first, a, b), jnp.where(first, b, a)], axis=0).astype(BF)


def final_kernel(own, far, far_2, near, near_2, out, chips):
    pos = position()
    first, chip = pos[1] == 0, pos[2]
    a, b = near[...].astype(F32), near_2[...].astype(F32)
    chips[chip] = own[...].astype(F32)
    chips[lax.rem(chip + 2 + pos[1], 4)] = far[...].astype(F32)
    chips[lax.rem(chip + 3 - pos[1], 4)] = far_2[...].astype(F32)
    chips[lax.rem(chip + 1, 4)] = jnp.concatenate(
        [jnp.where(first, a, b), jnp.where(first, b, a)], axis=0
    )
    total = ((chips[0] + chips[1]) + chips[2]) + chips[3]
    rows = []
    for core in range(2):
        part = total[core * SLOTS : (core + 1) * SLOTS, :]
        for q in range(PACK):
            at = PACK * LAT + q * ROPE
            rows.append(
                jnp.concatenate([part[:, q * LAT : (q + 1) * LAT], part[:, at : at + ROPE]], axis=1)
            )
    out[...] = jnp.concatenate(rows, axis=0).astype(BF)


def swap(value):
    return lax.ppermute(value, "co", [(0, 1), (1, 0)])


def turn_far(value):
    steps = [(2 * z + c, 2 * ((z + 2 - c) % 4) + c) for z in range(4) for c in range(2)]
    return lax.ppermute(value, EXP, steps)


def turn_near(value):
    return lax.ppermute(value, "zh", [(z, (z + 3) % 4) for z in range(4)])


def exchange(value):
    return lax.all_to_all(value, CTX, split_axis=0, concat_axis=0, tiled=True)


def shards(
    queries,
    key_latents,
    query_pos,
    value_up,
    out_proj,
    stream,
    norm_gain,
    expert_ids,
    gate_weights,
    w_gate,
    w_up,
    w_down,
    out_grad,
):
    ctx_count = lax.axis_size(CTX)
    exp_count = lax.axis_size("zh") * lax.axis_size("co")
    rows, width = stream.shape
    slots = ctx_count * SLOTS
    gain = norm_gain.reshape(width // 128, 128)
    hidden = w_gate.shape[2]

    key_count, key_width = key_latents.shape
    send, weight = call(
        functools.partial(prep_kernel, exp_count),
        [shape((slots, 3 * width), BF), shape((slots, rows), F32)],
        [expert_ids.T, gate_weights.T, stream, gain, out_grad, key_latents],
        58,
        flops=4 * slots * rows * width,
        scratch=[
            pltpu.VMEM((TOP, rows), jnp.int32),
            pltpu.VMEM((TOP, rows), F32),
            pltpu.VMEM((rows, width), BF),
            pltpu.VMEM(gain.shape, BF),
            pltpu.VMEM((rows, width), BF),
            pltpu.VMEM((key_count, key_width), BF),
            pltpu.SemaphoreType.DMA((6,)),
            pltpu.VMEM((slots, 3 * width), BF),
            pltpu.SemaphoreType.DMA((7 + PACK,)),
        ],
        far=range(6),
        far_out=(0,),
    )
    arrived = exchange(send.reshape(ctx_count, SLOTS, 3 * width)).reshape(slots, 3 * width)
    grads, mine = call(
        expert_kernel,
        [shape((slots, width), BF), shape((slots, width), BF)],
        [arrived, w_gate[0], w_up[0], w_down[0]],
        12,
        flops=10 * slots * width * hidden,
        scratch=[
            pltpu.VMEM((slots, width), BF),
            pltpu.SemaphoreType.DMA((4,)),
        ],
        far_out=(0, 1),
    )
    returned = exchange(grads.reshape(ctx_count, SLOTS, width))
    other = swap(mine)
    heads = queries.shape[1]
    flat = heads * rows
    half = slots * PACK
    wide = LAT + 4 * ROPE
    probs, latent_out, query_rows = call(
        scores_kernel,
        [
            shape((2 * PACK, slots, flat), BF),
            shape((LAT, flat), F32),
            shape((flat, wide), BF),
        ],
        [mine, other, jnp.transpose(queries, (1, 2, 0)), query_pos.reshape(1, rows)],
        14,
        flops=4 * half * flat * (key_width + LAT),
        scratch=[
            pltpu.VMEM((slots, width), BF),
            pltpu.VMEM((slots, width), BF),
            pltpu.VMEM((2 * PACK, slots, flat), F32),
            pltpu.VMEM((2 * PACK, slots, flat), BF),
            pltpu.VMEM((LAT, flat), F32),
            pltpu.VMEM((flat, wide), BF),
            pltpu.SemaphoreType.DMA((4 + 2 * PACK,)),
        ],
        far=(0, 1),
        far_out=(0, 1, 2),
    )
    (ordered,) = call(order_kernel, [shape((rows, 2 * slots), BF)], [weight], 4)
    returned, probs, latent_out, query_rows, ordered = lax.optimization_barrier(
        (returned, probs, latent_out, query_rows, ordered)
    )
    returned = returned.reshape(slots, width)

    (other_part,) = call(
        functools.partial(combine_kernel, 1),
        [shape((rows // 2, width), BF)],
        [returned, ordered],
        8,
    )
    received = swap(other_part)
    (keep,) = call(
        functools.partial(combine_kernel, 0),
        [shape((rows // 2, width), F32)],
        [returned, ordered],
        8,
    )
    piece = rows // 8
    own, near, far = call(
        pair_kernel,
        [shape((piece, width), BF), shape((piece, width), BF), shape((2 * piece, width), BF)],
        [keep, received],
        4,
    )
    near, far = turn_near(near), turn_far(far)
    own_grad, half_grad = call(
        stream_kernel,
        [shape((2 * piece, width), BF), shape((piece, width), BF)],
        [own, swap(own), far, swap(far), near, swap(near), stream, gain, out_grad],
        4,
    )
    near, far = turn_near(half_grad), turn_far(own_grad)
    stream_grad, latent_t, latent_rows, delta = call(
        latent_kernel,
        [
            shape((rows, width), BF),
            shape((LAT, flat), BF),
            shape((flat, LAT), BF),
            shape((1, flat), F32),
        ],
        [
            own_grad,
            far,
            swap(far),
            near,
            swap(near),
            out_proj,
            value_up,
            latent_out,
        ],
        8,
        flops=2 * flat * VHEAD * (width + LAT),
        scratch=[pltpu.VMEM((rows, width), BF), pltpu.SemaphoreType.DMA((1,))],
        far_out=(0,),
    )

    def back(side, keys):
        (key_part,) = call(
            functools.partial(back_kernel, side),
            [shape((slots, width), BF)],
            [keys, probs, latent_t, latent_rows, delta, query_rows],
            8,
            flops=2 * half * flat * (2 * LAT + key_width),
        )
        return key_part

    key_received = swap(back(1, other))
    key_mine = back(0, mine)
    (key_sum,) = call(
        add_kernel,
        [shape((slots, width), BF)],
        [key_mine, key_received],
        8,
        scratch=[pltpu.VMEM((slots, width), BF), pltpu.SemaphoreType.DMA((4,))],
        far_out=(0,),
    )
    key_parts = exchange(key_sum.reshape(ctx_count, SLOTS, width))
    (query_grad_t,) = call(
        query_kernel,
        [shape((heads, key_width, rows), BF)],
        [mine, other, probs, latent_t, delta],
        16,
        flops=4 * half * flat * (key_width + LAT),
    )
    key_parts, query_grad_t = lax.optimization_barrier((key_parts, query_grad_t))
    query_grad = jnp.transpose(query_grad_t, (2, 0, 1))
    (key_own,) = call(
        sum_kernel, [shape((SLOTS, width), BF)], [key_parts.reshape(slots, width)], 8
    )
    (key_chip,) = call(
        join_kernel, [shape((2 * SLOTS, width), BF)], [key_own, swap(key_own)], 4
    )
    far, near = turn_far(key_chip), turn_near(key_own)
    (key_grad,) = call(
        final_kernel,
        [shape((key_count, key_width), BF)],
        [key_chip, far, swap(far), near, swap(near)],
        4,
        scratch=[pltpu.VMEM((4, 2 * SLOTS, width), F32)],
    )
    return (stream_grad, query_grad, key_grad)


def solution(mesh):
    fine = Mesh(mesh.devices.reshape(4, 4, 2, 4, 2), ("y", "x", "zl", "zh", "co"))
    exp = EXP
    both = CTX + exp
    placed = (
        P(CTX, exp, None),
        P(CTX, None),
        P(CTX),
        P(exp, None, None),
        P(exp, None, None),
        P(CTX, None),
        P(),
        P(CTX, None),
        P(CTX, None),
        P(both, None, None),
        P(both, None, None),
        P(both, None, None),
        P(CTX, None),
    )
    return jax.shard_map(
        shards,
        mesh=fine,
        in_specs=placed,
        out_specs=(P(CTX, None), P(CTX, exp, None), P(CTX, None)),
        check_vma=False,
    )
```

profile of v0, /device:TPU:1, one launch (start us, length us, event | category | flops | bytes accessed | tf_op | source)
XLA Modules:
  0.0 162.6 jit_solution(8362179857279846387)
XLA Ops:
  0.6 4.4 %shard_map.148 = (bf16[256,6912]{1,0:T(8,128)(2,1)}, f32[256,128]{1,0:T(8,128)}) custom-call(s32[8,128]{1,0:T(8,128)} %bitcast.27, f32[8,128]{1,0:T(8,128)} %bitcast.28, bf16[128,2304]{1,0:T(8,128)(2,1)} %stream.1, bf16[18,128]{1,0:T(8,128)(2,1)} %bitcast.19, bf16[128,2304]{1,0:T(8,128)(2,1)} %out_grad.1, bf16[64,576]{1,0:T(8,128)(2,1)} %refs_5_.1), custom_call_target="tpu_custom_call" | custom-call | flops 301989888 | bytes 4936192 | tf_op jit(solution)/shard_map/pallas_call | solution.py:45
  5.0 53.2 %all_to_all.15 = bf16[32,8,6912]{2,1,0:T(8,128)(2,1)S(1)} all-to-all(bf16[32,8,6912]{2,1,0:T(8,128)(2,1)} %bitcast.26), channel_id=1, replica_groups=mesh['y'=4,'x'=4,'zl'=2,'zh'=4,'co'=2] {'y','x','zl'}, dimensions={0} | all-to-all | bytes 7077888 | tf_op jit(solution)/shard_map/all_to_all | solution.py:464
  58.3 4.4 %shard_map.149 = (bf16[256,2304]{1,0:T(8,128)(2,1)}, bf16[256,2304]{1,0:T(8,128)(2,1)S(1)}) custom-call(bf16[256,6912]{1,0:T(8,128)(2,1)S(1)} %bitcast.18, bf16[2304,512]{1,0:T(8,128)(2,1)S(1)} %bitcast.21, bf16[2304,512]{1,0:T(8,128)(2,1)S(1)} %bitcast.22, bf16[512,2304]{1,0:T(8,128)(2,1)S(1)} %bitcast.23), custom_call_target="tpu_custom_call" | custom-call | flops 3019898880 | bytes 12976128 | tf_op jit(solution)/shard_map/pallas_call | solution.py:45
  62.7 4.1 %all-to-all-start.1 = ((bf16[32,8,2304]{2,1,0:T(8,128)(2,1)}), bf16[32,8,2304]{2,1,0:T(8,128)(2,1)S(1)}, u32[]{:S(2)}, u32[]{:S(2)}) async-start(bf16[32,8,2304]{2,1,0:T(8,128)(2,1)} %bitcast.8), calls=%async_computation.1 | async-start | bytes 2359296 | tf_op jit(solution)/shard_map/all_to_all | solution.py:464
  66.8 1.9 %collective-permute-start = (bf16[256,2304]{1,0:T(8,128)(2,1)S(1)}, bf16[256,2304]{1,0:T(8,128)(2,1)S(1)}, u32[]{:S(2)}, u32[]{:S(2)}) collective-permute-start(bf16[256,2304]{1,0:T(8,128)(2,1)S(1)} %get-tuple-element.28.mine_far.keys.mine), channel_id=1, source_target_pairs={{0,1},{1,0},{2,3},{3,2},{4,5},{5,4},{6,7},{7,6},{8,9},{9,8},{10,11... | collective-permute-start | bytes 3538952 | tf_op jit(solution)/shard_map/ppermute | solution.py:451
  69.0 2.2 %collective-permute-done.other_far.keys.other = bf16[256,2304]{1,0:T(8,128)(2,1)S(1)} collective-permute-done((bf16[256,2304]{1,0:T(8,128)(2,1)S(1)}, bf16[256,2304]{1,0:T(8,128)(2,1)S(1)}, u32[]{:S(2)}, u32[]{:S(2)}) %collective-permute-start) | collective-permute-done | bytes 1179680 | tf_op jit(solution)/shard_map/ppermute | solution.py:451
  73.5 5.7 %shard_map.150 = (bf16[8,256,512]{2,1,0:T(8,128)(2,1)S(1)}, f32[512,512]{1,0:T(8,128)S(1)}, bf16[512,768]{1,0:T(8,128)(2,1)S(1)}) custom-call(bf16[256,2304]{1,0:T(8,128)(2,1)S(1)} %copy-done.8, bf16[256,2304]{1,0:T(8,128)(2,1)S(1)} %collective-permute-done.other_far.keys.other, bf16[4,576,128]{2,1,0:T(8,128)(2,1)S(1)} %bitcast.24, s32[1,128]{1,0:T(1,128)S(1)} %bitcast.25), custom_call_target="tpu_custom_call" | custom-call | flops 2281701376 | bytes 6881792 | tf_op jit(solution)/shard_map/pallas_call | solution.py:45
  82.2 1.9 %all-to-all-done.1 = bf16[32,8,2304]{2,1,0:T(8,128)(2,1)S(1)} async-done(((bf16[32,8,2304]{2,1,0:T(8,128)(2,1)}), bf16[32,8,2304]{2,1,0:T(8,128)(2,1)S(1)}, u32[]{:S(2)}, u32[]{:S(2)}) %all-to-all-start.1) | async-done | bytes 1179680 | tf_op jit(solution)/shard_map/all_to_all | solution.py:464
  84.7 3.0 %collective-permute-start.1 = (bf16[64,2304]{1,0:T(8,128)(2,1)S(1)}, bf16[64,2304]{1,0:T(8,128)(2,1)S(1)}, u32[]{:S(2)}, u32[]{:S(2)}) collective-permute-start(bf16[64,2304]{1,0:T(8,128)(2,1)S(1)} %shard_map.153), channel_id=1, source_target_pairs={{0,1},{1,0},{2,3},{3,2},{4,5},{5,4},{6,7},{7,6},{8,9},{9,8},{10,11... | collective-permute-start | bytes 884744 | tf_op jit(solution)/shard_map/ppermute | solution.py:451
  89.0 3.1 %collective-permute-start.3 = (bf16[32,2304]{1,0:T(8,128)(2,1)S(1)}, bf16[32,2304]{1,0:T(8,128)(2,1)S(1)}, u32[]{:S(2)}, u32[]{:S(2)}) collective-permute-start(bf16[32,2304]{1,0:T(8,128)(2,1)S(1)} %get-tuple-element.36), channel_id=1, source_target_pairs={{0,4},{1,3},{2,6},{3,5},{4,0},{5,7},{6,2},{7,1},{8,12},{9,11},{10,... | collective-permute-start | bytes 442376 | tf_op jit(solution)/shard_map/ppermute | solution.py:456
  92.0 2.4 %collective-permute-start.5 = (bf16[16,2304]{1,0:T(8,128)(2,1)S(1)}, bf16[16,2304]{1,0:T(8,128)(2,1)S(1)}, u32[]{:S(2)}, u32[]{:S(2)}) collective-permute-start(bf16[16,2304]{1,0:T(8,128)(2,1)S(1)} %get-tuple-element.37), channel_id=1, source_target_pairs={{0,6},{2,0},{4,2},{6,4},{1,7},{3,1},{5,3},{7,5},{8,14},{10,8},{12,... | collective-permute-start | bytes 221192 | tf_op jit(solution)/shard_map/ppermute | solution.py:460
  94.4 5.7 %collective-permute-done.3.far = bf16[32,2304]{1,0:T(8,128)(2,1)S(1)} collective-permute-done((bf16[32,2304]{1,0:T(8,128)(2,1)S(1)}, bf16[32,2304]{1,0:T(8,128)(2,1)S(1)}, u32[]{:S(2)}, u32[]{:S(2)}) %collective-permute-start.3) | collective-permute-done | bytes 147488 | tf_op jit(solution)/shard_map/ppermute | solution.py:456
  106.1 2.1 %collective-permute-start.9 = (bf16[16,2304]{1,0:T(8,128)(2,1)S(1)}, bf16[16,2304]{1,0:T(8,128)(2,1)S(1)}, u32[]{:S(2)}, u32[]{:S(2)}) collective-permute-start(bf16[16,2304]{1,0:T(8,128)(2,1)S(1)} %get-tuple-element.39), channel_id=1, source_target_pairs={{0,6},{2,0},{4,2},{6,4},{1,7},{3,1},{5,3},{7,5},{8,14},{10,8},{12,... | collective-permute-start | bytes 221192 | tf_op jit(solution)/shard_map/ppermute | solution.py:460
  108.2 3.9 %collective-permute-done.7.far = bf16[32,2304]{1,0:T(8,128)(2,1)S(1)} collective-permute-done((bf16[32,2304]{1,0:T(8,128)(2,1)S(1)}, bf16[32,2304]{1,0:T(8,128)(2,1)S(1)}, u32[]{:S(2)}, u32[]{:S(2)}) %collective-permute-start.7) | collective-permute-done | bytes 147488 | tf_op jit(solution)/shard_map/ppermute | solution.py:456
  112.1 4.0 %collective-permute-start.8 = (bf16[32,2304]{1,0:T(8,128)(2,1)S(1)}, bf16[32,2304]{1,0:T(8,128)(2,1)S(1)}, u32[]{:S(2)}, u32[]{:S(2)}) collective-permute-start(bf16[32,2304]{1,0:T(8,128)(2,1)S(1)} %collective-permute-done.7.far), channel_id=1, source_target_pairs={{0,1},{1,0},{2,3},{3,2},{4,5},{5,4},{6,7},{7,6},{8,9},{9,8},{10,11... | collective-permute-start | bytes 442376 | tf_op jit(solution)/shard_map/ppermute | solution.py:451
  117.5 2.1 %shard_map.156 = (bf16[128,2304]{1,0:T(8,128)(2,1)}, bf16[512,512]{1,0:T(8,128)(2,1)S(1)}, bf16[512,512]{1,0:T(8,128)(2,1)S(1)}, f32[1,512]{1,0:T(1,128)S(1)}) custom-call(bf16[32,2304]{1,0:T(8,128)(2,1)S(1)} %get-tuple-element.38.own, bf16[32,2304]{1,0:T(8,128)(2,1)S(1)} %collective-permute-done.7.far, bf16[32,2304]{1,0:T(8,128)(2,1)S(1)} %collective-permute-done.8.far_2, ...), custom_call_target="tpu_custom_call" | custom-call | flops 369098752 | bytes 6162432 | tf_op jit(solution)/shard_map/pallas_call | solution.py:45
  119.6 2.2 %shard_map.158 = bf16[256,2304]{1,0:T(8,128)(2,1)S(1)} custom-call(bf16[256,2304]{1,0:T(8,128)(2,1)S(1)} %copy-done.12, bf16[8,256,512]{2,1,0:T(8,128)(2,1)S(1)} %get-tuple-element.42.probs, bf16[512,512]{1,0:T(8,128)(2,1)S(1)} %get-tuple-element.43.latent_t, bf16[512,512]{1,0:T(8,128)(2,1)S(1)} %get-tuple-element.44.latent_rows, ...), custom_call_target="tpu_custom_call" | custom-call | flops 1677721600 | bytes 6293504 | tf_op jit(solution)/shard_map/pallas_call | solution.py:45
  122.1 2.2 %shard_map.157.left = bf16[256,2304]{1,0:T(8,128)(2,1)S(1)} custom-call(bf16[256,2304]{1,0:T(8,128)(2,1)S(1)} %copy-done.9, bf16[8,256,512]{2,1,0:T(8,128)(2,1)S(1)} %get-tuple-element.42.probs, bf16[512,512]{1,0:T(8,128)(2,1)S(1)} %get-tuple-element.43.latent_t, bf16[512,512]{1,0:T(8,128)(2,1)S(1)} %get-tuple-element.44.latent_rows, ...), custom_call_target="tpu_custom_call" | custom-call | flops 1677721600 | bytes 6293504 | tf_op jit(solution)/shard_map/pallas_call | solution.py:45
  125.8 4.2 %all-to-all-start.2 = ((bf16[32,8,2304]{2,1,0:T(8,128)(2,1)}), bf16[32,8,2304]{2,1,0:T(8,128)(2,1)S(1)}, u32[]{:S(2)}, u32[]{:S(2)}) async-start(bf16[32,8,2304]{2,1,0:T(8,128)(2,1)} %bitcast.12), calls=%async_computation.2 | async-start | bytes 2359296 | tf_op jit(solution)/shard_map/all_to_all | solution.py:464
  133.6 6.0 %shard_map.160 = bf16[4,576,128]{2,1,0:T(8,128)(2,1)} custom-call(bf16[256,2304]{1,0:T(8,128)(2,1)S(1)} %copy-done.10, bf16[256,2304]{1,0:T(8,128)(2,1)S(1)} %copy-done.13, bf16[8,256,512]{2,1,0:T(8,128)(2,1)S(1)} %get-tuple-element.42.probs, bf16[512,512]{1,0:T(8,128)(2,1)S(1)} %copy-done.6, f32[1,512]{1,0:T(1,128)S(1)} %get-tuple-element.45.delta), custom_call_target="tpu_custom_call" | custom-call | flops 2281701376 | bytes 5572608 | tf_op jit(solution)/shard_map/pallas_call | solution.py:45
  139.6 8.8 %all-to-all-done.2 = bf16[32,8,2304]{2,1,0:T(8,128)(2,1)S(1)} async-done(((bf16[32,8,2304]{2,1,0:T(8,128)(2,1)}), bf16[32,8,2304]{2,1,0:T(8,128)(2,1)S(1)}, u32[]{:S(2)}, u32[]{:S(2)}) %all-to-all-start.2) | async-done | bytes 1179680 | tf_op jit(solution)/shard_map/all_to_all | solution.py:464
  152.9 1.9 %collective-permute-start.15 = (bf16[8,2304]{1,0:T(8,128)(2,1)S(1)}, bf16[8,2304]{1,0:T(8,128)(2,1)S(1)}, u32[]{:S(2)}, u32[]{:S(2)}) collective-permute-start(bf16[8,2304]{1,0:T(8,128)(2,1)S(1)} %shard_map.161.own), channel_id=1, source_target_pairs={{0,6},{2,0},{4,2},{6,4},{1,7},{3,1},{5,3},{7,5},{8,14},{10,8},{12,... | collective-permute-start | bytes 110600 | tf_op jit(solution)/shard_map/ppermute | solution.py:460
  154.8 2.5 %collective-permute-done.13.far = bf16[16,2304]{1,0:T(8,128)(2,1)S(1)} collective-permute-done((bf16[16,2304]{1,0:T(8,128)(2,1)S(1)}, bf16[16,2304]{1,0:T(8,128)(2,1)S(1)}, u32[]{:S(2)}, u32[]{:S(2)}) %collective-permute-start.13) | collective-permute-done | bytes 73760 | tf_op jit(solution)/shard_map/ppermute | solution.py:456
  157.3 2.9 %collective-permute-start.14 = (bf16[16,2304]{1,0:T(8,128)(2,1)S(1)}, bf16[16,2304]{1,0:T(8,128)(2,1)S(1)}, u32[]{:S(2)}, u32[]{:S(2)}) collective-permute-start(bf16[16,2304]{1,0:T(8,128)(2,1)S(1)} %collective-permute-done.13.far), channel_id=1, source_target_pairs={{0,1},{1,0},{2,3},{3,2},{4,5},{5,4},{6,7},{7,6},{8,9},{9,8},{10,11... | collective-permute-start | bytes 221192 | tf_op jit(solution)/shard_map/ppermute | solution.py:451
  (79 shorter events, 27.0 us)
Async XLA Ops:
  5.0 53.2 %copy-start.19 = (bf16[1,2304,512]{2,1,0:T(8,128)(2,1)S(1)}, bf16[1,2304,512]{2,1,0:T(8,128)(2,1)}, u32[]{:S(2)}) copy-start(bf16[1,2304,512]{2,1,0:T(8,128)(2,1)} %param.22) | copy-start | bytes 7077892
  5.0 53.2 %copy-start.20 = (bf16[1,2304,512]{2,1,0:T(8,128)(2,1)S(1)}, bf16[1,2304,512]{2,1,0:T(8,128)(2,1)}, u32[]{:S(2)}) copy-start(bf16[1,2304,512]{2,1,0:T(8,128)(2,1)} %param.23) | copy-start | bytes 7077892
  5.0 53.2 %copy-start.21 = (bf16[1,512,2304]{2,1,0:T(8,128)(2,1)S(1)}, bf16[1,512,2304]{2,1,0:T(8,128)(2,1)}, u32[]{:S(2)}) copy-start(bf16[1,512,2304]{2,1,0:T(8,128)(2,1)} %param.24) | copy-start | bytes 7077892
  62.7 21.4 %all-to-all-start.1 = ((bf16[32,8,2304]{2,1,0:T(8,128)(2,1)}), bf16[32,8,2304]{2,1,0:T(8,128)(2,1)S(1)}, u32[]{:S(2)}, u32[]{:S(2)}) async-start(bf16[32,8,2304]{2,1,0:T(8,128)(2,1)} %bitcast.8), calls=%async_computation.1 | async-start | bytes 2359296 | tf_op jit(solution)/shard_map/all_to_all | solution.py:464
  66.8 4.4 %collective-permute-start = (bf16[256,2304]{1,0:T(8,128)(2,1)S(1)}, bf16[256,2304]{1,0:T(8,128)(2,1)S(1)}, u32[]{:S(2)}, u32[]{:S(2)}) collective-permute-start(bf16[256,2304]{1,0:T(8,128)(2,1)S(1)} %get-tuple-element.28.mine_far.keys.mine), channel_id=1, source_target_pairs={{0,1},{1,0},{2,3},{3,2},{4,5},{5,4},{6,7},{7,6},{8,9},{9,8},{10,11... | collective-permute-start | bytes 3538952 | tf_op jit(solution)/shard_map/ppermute | solution.py:451
  84.1 33.3 %copy-start.15 = (f32[512,512]{1,0:T(8,128)S(1)}, f32[512,512]{1,0:T(8,128)}, u32[]{:S(2)}) copy-start(f32[512,512]{1,0:T(8,128)} %copy-done.14) | copy-start | bytes 3145732
  84.7 4.2 %collective-permute-start.1 = (bf16[64,2304]{1,0:T(8,128)(2,1)S(1)}, bf16[64,2304]{1,0:T(8,128)(2,1)S(1)}, u32[]{:S(2)}, u32[]{:S(2)}) collective-permute-start(bf16[64,2304]{1,0:T(8,128)(2,1)S(1)} %shard_map.153), channel_id=1, source_target_pairs={{0,1},{1,0},{2,3},{3,2},{4,5},{5,4},{6,7},{7,6},{8,9},{9,8},{10,11... | collective-permute-start | bytes 884744 | tf_op jit(solution)/shard_map/ppermute | solution.py:451
  87.7 29.7 %copy-start.16 = (bf16[4,512,128]{2,1,0:T(8,128)(2,1)S(1)}, bf16[4,512,128]{2,1,0:T(8,128)(2,1)}, u32[]{:S(2)}) copy-start(bf16[4,512,128]{2,1,0:T(8,128)(2,1)} %value_up.1) | copy-start | bytes 1572868
  89.0 11.2 %collective-permute-start.3 = (bf16[32,2304]{1,0:T(8,128)(2,1)S(1)}, bf16[32,2304]{1,0:T(8,128)(2,1)S(1)}, u32[]{:S(2)}, u32[]{:S(2)}) collective-permute-start(bf16[32,2304]{1,0:T(8,128)(2,1)S(1)} %get-tuple-element.36), channel_id=1, source_target_pairs={{0,4},{1,3},{2,6},{3,5},{4,0},{5,7},{6,2},{7,1},{8,12},{9,11},{10,... | collective-permute-start | bytes 442376 | tf_op jit(solution)/shard_map/ppermute | solution.py:456
  92.0 10.8 %collective-permute-start.5 = (bf16[16,2304]{1,0:T(8,128)(2,1)S(1)}, bf16[16,2304]{1,0:T(8,128)(2,1)S(1)}, u32[]{:S(2)}, u32[]{:S(2)}) collective-permute-start(bf16[16,2304]{1,0:T(8,128)(2,1)S(1)} %get-tuple-element.37), channel_id=1, source_target_pairs={{0,6},{2,0},{4,2},{6,4},{1,7},{3,1},{5,3},{7,5},{8,14},{10,8},{12,... | collective-permute-start | bytes 221192 | tf_op jit(solution)/shard_map/ppermute | solution.py:460
  100.1 4.1 %collective-permute-start.4 = (bf16[32,2304]{1,0:T(8,128)(2,1)S(1)}, bf16[32,2304]{1,0:T(8,128)(2,1)S(1)}, u32[]{:S(2)}, u32[]{:S(2)}) collective-permute-start(bf16[32,2304]{1,0:T(8,128)(2,1)S(1)} %collective-permute-done.3.far), channel_id=1, source_target_pairs={{0,1},{1,0},{2,3},{3,2},{4,5},{5,4},{6,7},{7,6},{8,9},{9,8},{10,11... | collective-permute-start | bytes 442376 | tf_op jit(solution)/shard_map/ppermute | solution.py:451
  101.4 1.9 %collective-permute-start.2 = (bf16[16,2304]{1,0:T(8,128)(2,1)S(1)}, bf16[16,2304]{1,0:T(8,128)(2,1)S(1)}, u32[]{:S(2)}, u32[]{:S(2)}) collective-permute-start(bf16[16,2304]{1,0:T(8,128)(2,1)S(1)} %get-tuple-element.35.own), channel_id=1, source_target_pairs={{0,1},{1,0},{2,3},{3,2},{4,5},{5,4},{6,7},{7,6},{8,9},{9,8},{10,11... | collective-permute-start | bytes 221192 | tf_op jit(solution)/shard_map/ppermute | solution.py:451
  102.8 1.4 collective-permute-start.6
  104.5 7.6 %collective-permute-start.7 = (bf16[32,2304]{1,0:T(8,128)(2,1)S(1)}, bf16[32,2304]{1,0:T(8,128)(2,1)S(1)}, u32[]{:S(2)}, u32[]{:S(2)}) collective-permute-start(bf16[32,2304]{1,0:T(8,128)(2,1)S(1)} %get-tuple-element.38.own), channel_id=1, source_target_pairs={{0,4},{1,3},{2,6},{3,5},{4,0},{5,7},{6,2},{7,1},{8,12},{9,11},{10,... | collective-permute-start | bytes 442376 | tf_op jit(solution)/shard_map/ppermute | solution.py:456
  106.1 10.1 %collective-permute-start.9 = (bf16[16,2304]{1,0:T(8,128)(2,1)S(1)}, bf16[16,2304]{1,0:T(8,128)(2,1)S(1)}, u32[]{:S(2)}, u32[]{:S(2)}) collective-permute-start(bf16[16,2304]{1,0:T(8,128)(2,1)S(1)} %get-tuple-element.39), channel_id=1, source_target_pairs={{0,6},{2,0},{4,2},{6,4},{1,7},{3,1},{5,3},{7,5},{8,14},{10,8},{12,... | collective-permute-start | bytes 221192 | tf_op jit(solution)/shard_map/ppermute | solution.py:460
  112.1 5.3 %collective-permute-start.8 = (bf16[32,2304]{1,0:T(8,128)(2,1)S(1)}, bf16[32,2304]{1,0:T(8,128)(2,1)S(1)}, u32[]{:S(2)}, u32[]{:S(2)}) collective-permute-start(bf16[32,2304]{1,0:T(8,128)(2,1)S(1)} %collective-permute-done.7.far), channel_id=1, source_target_pairs={{0,1},{1,0},{2,3},{3,2},{4,5},{5,4},{6,7},{7,6},{8,9},{9,8},{10,11... | collective-permute-start | bytes 442376 | tf_op jit(solution)/shard_map/ppermute | solution.py:451
  116.2 1.3 collective-permute-start.10
  121.8 2.9 %collective-permute-start.11 = (bf16[256,2304]{1,0:T(8,128)(2,1)S(1)}, bf16[256,2304]{1,0:T(8,128)(2,1)S(1)}, u32[]{:S(2)}, u32[]{:S(2)}) collective-permute-start(bf16[256,2304]{1,0:T(8,128)(2,1)S(1)} %shard_map.158), channel_id=1, source_target_pairs={{0,1},{1,0},{2,3},{3,2},{4,5},{5,4},{6,7},{7,6},{8,9},{9,8},{10,11... | collective-permute-start | bytes 3538952 | tf_op jit(solution)/shard_map/ppermute | solution.py:451
  125.8 22.5 %all-to-all-start.2 = ((bf16[32,8,2304]{2,1,0:T(8,128)(2,1)}), bf16[32,8,2304]{2,1,0:T(8,128)(2,1)S(1)}, u32[]{:S(2)}, u32[]{:S(2)}) async-start(bf16[32,8,2304]{2,1,0:T(8,128)(2,1)} %bitcast.12), calls=%async_computation.2 | async-start | bytes 2359296 | tf_op jit(solution)/shard_map/all_to_all | solution.py:464
  148.5 2.6 %collective-permute-start.12 = (bf16[8,2304]{1,0:T(8,128)(2,1)S(1)}, bf16[8,2304]{1,0:T(8,128)(2,1)S(1)}, u32[]{:S(2)}, u32[]{:S(2)}) collective-permute-start(bf16[8,2304]{1,0:T(8,128)(2,1)S(1)} %shard_map.161.own), channel_id=1, source_target_pairs={{0,1},{1,0},{2,3},{3,2},{4,5},{5,4},{6,7},{7,6},{8,9},{9,8},{10,11... | collective-permute-start | bytes 110600 | tf_op jit(solution)/shard_map/ppermute | solution.py:451
  151.1 6.2 %collective-permute-start.13 = (bf16[16,2304]{1,0:T(8,128)(2,1)S(1)}, bf16[16,2304]{1,0:T(8,128)(2,1)S(1)}, u32[]{:S(2)}, u32[]{:S(2)}) collective-permute-start(bf16[16,2304]{1,0:T(8,128)(2,1)S(1)} %shard_map.162.own), channel_id=1, source_target_pairs={{0,4},{1,3},{2,6},{3,5},{4,0},{5,7},{6,2},{7,1},{8,12},{9,11},{10,... | collective-permute-start | bytes 221192 | tf_op jit(solution)/shard_map/ppermute | solution.py:456
  152.9 7.3 %collective-permute-start.15 = (bf16[8,2304]{1,0:T(8,128)(2,1)S(1)}, bf16[8,2304]{1,0:T(8,128)(2,1)S(1)}, u32[]{:S(2)}, u32[]{:S(2)}) collective-permute-start(bf16[8,2304]{1,0:T(8,128)(2,1)S(1)} %shard_map.161.own), channel_id=1, source_target_pairs={{0,6},{2,0},{4,2},{6,4},{1,7},{3,1},{5,3},{7,5},{8,14},{10,8},{12,... | collective-permute-start | bytes 110600 | tf_op jit(solution)/shard_map/ppermute | solution.py:460
  157.3 4.6 %collective-permute-start.14 = (bf16[16,2304]{1,0:T(8,128)(2,1)S(1)}, bf16[16,2304]{1,0:T(8,128)(2,1)S(1)}, u32[]{:S(2)}, u32[]{:S(2)}) collective-permute-start(bf16[16,2304]{1,0:T(8,128)(2,1)S(1)} %collective-permute-done.13.far), channel_id=1, source_target_pairs={{0,1},{1,0},{2,3},{3,2},{4,5},{5,4},{6,7},{7,6},{8,9},{9,8},{10,11... | collective-permute-start | bytes 221192 | tf_op jit(solution)/shard_map/ppermute | solution.py:451
  160.2 1.7 %collective-permute-start.16 = (bf16[8,2304]{1,0:T(8,128)(2,1)S(1)}, bf16[8,2304]{1,0:T(8,128)(2,1)S(1)}, u32[]{:S(2)}, u32[]{:S(2)}) collective-permute-start(bf16[8,2304]{1,0:T(8,128)(2,1)S(1)} %collective-permute-done.15.near), channel_id=1, source_target_pairs={{0,1},{1,0},{2,3},{3,2},{4,5},{5,4},{6,7},{7,6},{8,9},{9,8},{10,11... | collective-permute-start | bytes 110600 | tf_op jit(solution)/shard_map/ppermute | solution.py:451
  (19 other events, 147.3 us)
where the time goes:
time: 163 us
  blocking collectives  53.2 us (33%)
  starting transfers between devices  37.6 us (23%)
  waiting for transfers between devices  31.4 us (19%)
  Pallas kernels  30.6 us (19%)
  local copies, waits for them, and re-layouts  8.9 us (5%)
    all_to_all x1, blocking collectives, exchange(): return lax.all_to_all(value, CTX, split_axis=0, concat_axis=0, tiled=True)  53.2 us
    pallas_call x16, Pallas kernels, call(): pl.pallas_call(body, out_shape=tuple(outs), in_specs=[place(i in far) for...  30.6 us
    ppermute x11, starting transfers between devices, swap(): return lax.ppermute(value, 'co', [(0, 1), (1, 0)])  16.6 us
    ppermute x3, waiting for transfers between devices, turn_far(): return lax.ppermute(value, EXP, steps)  12.2 us
    all_to_all x2, waiting for transfers between devices, exchange(): return lax.all_to_all(value, CTX, split_axis=0, concat_axis=0, tiled=True)  10.7 us
    unnamed x48, local copies, waits for them, and re-layouts  8.9 us
    all_to_all x2, starting transfers between devices, exchange(): return lax.all_to_all(value, CTX, split_axis=0, concat_axis=0, tiled=True)  8.25 us
    ppermute x11, waiting for transfers between devices, swap(): return lax.ppermute(value, 'co', [(0, 1), (1, 0)])  7.11 us
  transfers between devices with their start and end apart: 19, of which 13 were waited for; matrix products, arithmetic and copies ran while one was open for 0% of the time, Pallas kernels for 9%

commit v1 on v0

--- a/solution.py
+++ b/solution.py
@@ -85,13 +85,31 @@
         pltpu.make_async_copy(source, target, arrived.at[i])
         for i, (source, target) in enumerate(zip(far, held))
     ]
-    for copy in copies:
-        copy.start()
+    for i in (5, 0, 1, 4, 2, 3):
+        copies[i].start()
     ids, gates, stream, gain, out_grad, keys = held
+    rows, width = stream.shape
+    slots = weight.shape[0]
+    copies[5].wait()
+    count = keys.shape[0]
+    row = lax.broadcasted_iota(jnp.int32, (SLOTS, count), 0)
+    key = lax.broadcasted_iota(jnp.int32, (SLOTS, count), 1)
+    parts, ropes = [], []
+    for q in range(PACK):
+        wanted = pos[1] * (count // 2) + q * SLOTS + row
+        pick = jnp.where(key == wanted, 1.0, 0.0).astype(BF)
+        parts.append(dot(pick, keys[:, :LAT]))
+        ropes.append(dot(pick, keys[:, LAT:]))
+    parts.append(jnp.concatenate(ropes, axis=1))
+    at = 2 * width
+    for part in parts:
+        wide = part.shape[1]
+        part = jnp.broadcast_to(part[None], (slots // SLOTS, SLOTS, wide))
+        send[:, at : at + wide] = part.reshape(slots, wide).astype(BF)
+        leave(at, wide)
+        at += wide
     copies[0].wait()
     copies[1].wait()
-    rows, width = stream.shape
-    slots = weight.shape[0]
     place = lax.broadcasted_iota(jnp.int32, (slots, rows), 0)
     expert = (place // SLOTS) * exp_count + pos[0]
     member = jnp.zeros((slots, rows), F32)
@@ -113,24 +131,6 @@
     for c in range(0, width, step):
         send[:, width + c : width + c + step] = dot(select, out_grad[:, c : c + step]).astype(BF)
         leave(width + c, step)
-    copies[5].wait()
-    count = keys.shape[0]
-    row = lax.broadcasted_iota(jnp.int32, (SLOTS, count), 0)
-    key = lax.broadcasted_iota(jnp.int32, (SLOTS, count), 1)
-    parts, ropes = [], []
-    for q in range(PACK):
-        wanted = pos[1] * (count // 2) + q * SLOTS + row
-        pick = jnp.where(key == wanted, 1.0, 0.0).astype(BF)
-        parts.append(dot(pick, keys[:, :LAT]))
-        ropes.append(dot(pick, keys[:, LAT:]))
-    parts.append(jnp.concatenate(ropes, axis=1))
-    at = 2 * width
-    for part in parts:
-        wide = part.shape[1]
-        part = jnp.broadcast_to(part[None], (slots // SLOTS, SLOTS, wide))
-        send[:, at : at + wide] = part.reshape(slots, wide).astype(BF)
-        leave(at, wide)
-        at += wide
     copies[2].wait()
     copies[3].wait()
     stream_f = stream[...].astype(F32)

time: 163 us -> 163 us (level)
  no operation moved by 1% of the time
where the time goes in v1:
time: 163 us; the launch traced here: 162 us
  blocking collectives  53.2 us (33%)
  starting transfers between devices  37.6 us (23%)
  waiting for transfers between devices  31.4 us (19%)
  Pallas kernels  30.5 us (19%)
  local copies, waits for them, and re-layouts  8.9 us (5%)
    all_to_all x1, blocking collectives, exchange(): return lax.all_to_all(value, CTX, split_axis=0, concat_axis=0, tiled=True)  53.2 us
    pallas_call x16, Pallas kernels, call(): pl.pallas_call(body, out_shape=tuple(outs), in_specs=[place(i in far) for...  30.5 us
    ppermute x11, starting transfers between devices, swap(): return lax.ppermute(value, 'co', [(0, 1), (1, 0)])  16.6 us
    ppermute x3, waiting for transfers between devices, turn_far(): return lax.ppermute(value, EXP, steps)  12.2 us
    all_to_all x2, waiting for transfers between devices, exchange(): return lax.all_to_all(value, CTX, split_axis=0, concat_axis=0, tiled=True)  10.7 us
    unnamed x48, local copies, waits for them, and re-layouts  8.9 us
    all_to_all x2, starting transfers between devices, exchange(): return lax.all_to_all(value, CTX, split_axis=0, concat_axis=0, tiled=True)  8.25 us
    ppermute x11, waiting for transfers between devices, swap(): return lax.ppermute(value, 'co', [(0, 1), (1, 0)])  7.1 us
  transfers between devices with their start and end apart: 19, of which 13 were waited for; matrix products, arithmetic and copies ran while one was open for 0% of the time, Pallas kernels for 9%

profile of v1, /device:TPU:1, one launch (start us, length us, event | category | flops | bytes accessed | tf_op | source)
XLA Modules:
  0.0 162.5 jit_solution(2914286907803165493)
XLA Ops:
  0.6 4.3 %shard_map.148 = (bf16[256,6912]{1,0:T(8,128)(2,1)}, f32[256,128]{1,0:T(8,128)}) custom-call(s32[8,128]{1,0:T(8,128)} %bitcast.27, f32[8,128]{1,0:T(8,128)} %bitcast.28, bf16[128,2304]{1,0:T(8,128)(2,1)} %stream.1, bf16[18,128]{1,0:T(8,128)(2,1)} %bitcast.19, bf16[128,2304]{1,0:T(8,128)(2,1)} %out_grad.1, bf16[64,576]{1,0:T(8,128)(2,1)} %refs_5_.1), custom_call_target="tpu_custom_call" | custom-call | flops 301989888 | bytes 4936192 | tf_op jit(solution)/shard_map/pallas_call | solution.py:45
  4.9 53.2 %all_to_all.15 = bf16[32,8,6912]{2,1,0:T(8,128)(2,1)S(1)} all-to-all(bf16[32,8,6912]{2,1,0:T(8,128)(2,1)} %bitcast.26), channel_id=1, replica_groups=mesh['y'=4,'x'=4,'zl'=2,'zh'=4,'co'=2] {'y','x','zl'}, dimensions={0} | all-to-all | bytes 7077888 | tf_op jit(solution)/shard_map/all_to_all | solution.py:464
  58.1 4.4 %shard_map.149 = (bf16[256,2304]{1,0:T(8,128)(2,1)}, bf16[256,2304]{1,0:T(8,128)(2,1)S(1)}) custom-call(bf16[256,6912]{1,0:T(8,128)(2,1)S(1)} %bitcast.18, bf16[2304,512]{1,0:T(8,128)(2,1)S(1)} %bitcast.21, bf16[2304,512]{1,0:T(8,128)(2,1)S(1)} %bitcast.22, bf16[512,2304]{1,0:T(8,128)(2,1)S(1)} %bitcast.23), custom_call_target="tpu_custom_call" | custom-call | flops 3019898880 | bytes 12976128 | tf_op jit(solution)/shard_map/pallas_call | solution.py:45
  62.6 4.1 %all-to-all-start.1 = ((bf16[32,8,2304]{2,1,0:T(8,128)(2,1)}), bf16[32,8,2304]{2,1,0:T(8,128)(2,1)S(1)}, u32[]{:S(2)}, u32[]{:S(2)}) async-start(bf16[32,8,2304]{2,1,0:T(8,128)(2,1)} %bitcast.8), calls=%async_computation.1 | async-start | bytes 2359296 | tf_op jit(solution)/shard_map/all_to_all | solution.py:464
  66.7 1.9 %collective-permute-start = (bf16[256,2304]{1,0:T(8,128)(2,1)S(1)}, bf16[256,2304]{1,0:T(8,128)(2,1)S(1)}, u32[]{:S(2)}, u32[]{:S(2)}) collective-permute-start(bf16[256,2304]{1,0:T(8,128)(2,1)S(1)} %get-tuple-element.28.mine_far.keys.mine), channel_id=1, source_target_pairs={{0,1},{1,0},{2,3},{3,2},{4,5},{5,4},{6,7},{7,6},{8,9},{9,8},{10,11... | collective-permute-start | bytes 3538952 | tf_op jit(solution)/shard_map/ppermute | solution.py:451
  68.8 2.2 %collective-permute-done.other_far.keys.other = bf16[256,2304]{1,0:T(8,128)(2,1)S(1)} collective-permute-done((bf16[256,2304]{1,0:T(8,128)(2,1)S(1)}, bf16[256,2304]{1,0:T(8,128)(2,1)S(1)}, u32[]{:S(2)}, u32[]{:S(2)}) %collective-permute-start) | collective-permute-done | bytes 1179680 | tf_op jit(solution)/shard_map/ppermute | solution.py:451
  73.4 5.7 %shard_map.150 = (bf16[8,256,512]{2,1,0:T(8,128)(2,1)S(1)}, f32[512,512]{1,0:T(8,128)S(1)}, bf16[512,768]{1,0:T(8,128)(2,1)S(1)}) custom-call(bf16[256,2304]{1,0:T(8,128)(2,1)S(1)} %copy-done.8, bf16[256,2304]{1,0:T(8,128)(2,1)S(1)} %collective-permute-done.other_far.keys.other, bf16[4,576,128]{2,1,0:T(8,128)(2,1)S(1)} %bitcast.24, s32[1,128]{1,0:T(1,128)S(1)} %bitcast.25), custom_call_target="tpu_custom_call" | custom-call | flops 2281701376 | bytes 6881792 | tf_op jit(solution)/shard_map/pallas_call | solution.py:45
  82.1 1.9 %all-to-all-done.1 = bf16[32,8,2304]{2,1,0:T(8,128)(2,1)S(1)} async-done(((bf16[32,8,2304]{2,1,0:T(8,128)(2,1)}), bf16[32,8,2304]{2,1,0:T(8,128)(2,1)S(1)}, u32[]{:S(2)}, u32[]{:S(2)}) %all-to-all-start.1) | async-done | bytes 1179680 | tf_op jit(solution)/shard_map/all_to_all | solution.py:464
  84.5 3.0 %collective-permute-start.1 = (bf16[64,2304]{1,0:T(8,128)(2,1)S(1)}, bf16[64,2304]{1,0:T(8,128)(2,1)S(1)}, u32[]{:S(2)}, u32[]{:S(2)}) collective-permute-start(bf16[64,2304]{1,0:T(8,128)(2,1)S(1)} %shard_map.153), channel_id=1, source_target_pairs={{0,1},{1,0},{2,3},{3,2},{4,5},{5,4},{6,7},{7,6},{8,9},{9,8},{10,11... | collective-permute-start | bytes 884744 | tf_op jit(solution)/shard_map/ppermute | solution.py:451
  88.8 3.1 %collective-permute-start.3 = (bf16[32,2304]{1,0:T(8,128)(2,1)S(1)}, bf16[32,2304]{1,0:T(8,128)(2,1)S(1)}, u32[]{:S(2)}, u32[]{:S(2)}) collective-permute-start(bf16[32,2304]{1,0:T(8,128)(2,1)S(1)} %get-tuple-element.36), channel_id=1, source_target_pairs={{0,4},{1,3},{2,6},{3,5},{4,0},{5,7},{6,2},{7,1},{8,12},{9,11},{10,... | collective-permute-start | bytes 442376 | tf_op jit(solution)/shard_map/ppermute | solution.py:456
  91.9 2.4 %collective-permute-start.5 = (bf16[16,2304]{1,0:T(8,128)(2,1)S(1)}, bf16[16,2304]{1,0:T(8,128)(2,1)S(1)}, u32[]{:S(2)}, u32[]{:S(2)}) collective-permute-start(bf16[16,2304]{1,0:T(8,128)(2,1)S(1)} %get-tuple-element.37), channel_id=1, source_target_pairs={{0,6},{2,0},{4,2},{6,4},{1,7},{3,1},{5,3},{7,5},{8,14},{10,8},{12,... | collective-permute-start | bytes 221192 | tf_op jit(solution)/shard_map/ppermute | solution.py:460
  94.3 5.7 %collective-permute-done.3.far = bf16[32,2304]{1,0:T(8,128)(2,1)S(1)} collective-permute-done((bf16[32,2304]{1,0:T(8,128)(2,1)S(1)}, bf16[32,2304]{1,0:T(8,128)(2,1)S(1)}, u32[]{:S(2)}, u32[]{:S(2)}) %collective-permute-start.3) | collective-permute-done | bytes 147488 | tf_op jit(solution)/shard_map/ppermute | solution.py:456
  106.0 2.1 %collective-permute-start.9 = (bf16[16,2304]{1,0:T(8,128)(2,1)S(1)}, bf16[16,2304]{1,0:T(8,128)(2,1)S(1)}, u32[]{:S(2)}, u32[]{:S(2)}) collective-permute-start(bf16[16,2304]{1,0:T(8,128)(2,1)S(1)} %get-tuple-element.39), channel_id=1, source_target_pairs={{0,6},{2,0},{4,2},{6,4},{1,7},{3,1},{5,3},{7,5},{8,14},{10,8},{12,... | collective-permute-start | bytes 221192 | tf_op jit(solution)/shard_map/ppermute | solution.py:460
  108.1 3.9 %collective-permute-done.7.far = bf16[32,2304]{1,0:T(8,128)(2,1)S(1)} collective-permute-done((bf16[32,2304]{1,0:T(8,128)(2,1)S(1)}, bf16[32,2304]{1,0:T(8,128)(2,1)S(1)}, u32[]{:S(2)}, u32[]{:S(2)}) %collective-permute-start.7) | collective-permute-done | bytes 147488 | tf_op jit(solution)/shard_map/ppermute | solution.py:456
  112.0 4.0 %collective-permute-start.8 = (bf16[32,2304]{1,0:T(8,128)(2,1)S(1)}, bf16[32,2304]{1,0:T(8,128)(2,1)S(1)}, u32[]{:S(2)}, u32[]{:S(2)}) collective-permute-start(bf16[32,2304]{1,0:T(8,128)(2,1)S(1)} %collective-permute-done.7.far), channel_id=1, source_target_pairs={{0,1},{1,0},{2,3},{3,2},{4,5},{5,4},{6,7},{7,6},{8,9},{9,8},{10,11... | collective-permute-start | bytes 442376 | tf_op jit(solution)/shard_map/ppermute | solution.py:451
  117.3 2.1 %shard_map.156 = (bf16[128,2304]{1,0:T(8,128)(2,1)}, bf16[512,512]{1,0:T(8,128)(2,1)S(1)}, bf16[512,512]{1,0:T(8,128)(2,1)S(1)}, f32[1,512]{1,0:T(1,128)S(1)}) custom-call(bf16[32,2304]{1,0:T(8,128)(2,1)S(1)} %get-tuple-element.38.own, bf16[32,2304]{1,0:T(8,128)(2,1)S(1)} %collective-permute-done.7.far, bf16[32,2304]{1,0:T(8,128)(2,1)S(1)} %collective-permute-done.8.far_2, ...), custom_call_target="tpu_custom_call" | custom-call | flops 369098752 | bytes 6162432 | tf_op jit(solution)/shard_map/pallas_call | solution.py:45
  119.5 2.2 %shard_map.158 = bf16[256,2304]{1,0:T(8,128)(2,1)S(1)} custom-call(bf16[256,2304]{1,0:T(8,128)(2,1)S(1)} %copy-done.12, bf16[8,256,512]{2,1,0:T(8,128)(2,1)S(1)} %get-tuple-element.42.probs, bf16[512,512]{1,0:T(8,128)(2,1)S(1)} %get-tuple-element.43.latent_t, bf16[512,512]{1,0:T(8,128)(2,1)S(1)} %get-tuple-element.44.latent_rows, ...), custom_call_target="tpu_custom_call" | custom-call | flops 1677721600 | bytes 6293504 | tf_op jit(solution)/shard_map/pallas_call | solution.py:45
  121.9 2.2 %shard_map.157.left = bf16[256,2304]{1,0:T(8,128)(2,1)S(1)} custom-call(bf16[256,2304]{1,0:T(8,128)(2,1)S(1)} %copy-done.9, bf16[8,256,512]{2,1,0:T(8,128)(2,1)S(1)} %get-tuple-element.42.probs, bf16[512,512]{1,0:T(8,128)(2,1)S(1)} %get-tuple-element.43.latent_t, bf16[512,512]{1,0:T(8,128)(2,1)S(1)} %get-tuple-element.44.latent_rows, ...), custom_call_target="tpu_custom_call" | custom-call | flops 1677721600 | bytes 6293504 | tf_op jit(solution)/shard_map/pallas_call | solution.py:45
  125.7 4.2 %all-to-all-start.2 = ((bf16[32,8,2304]{2,1,0:T(8,128)(2,1)}), bf16[32,8,2304]{2,1,0:T(8,128)(2,1)S(1)}, u32[]{:S(2)}, u32[]{:S(2)}) async-start(bf16[32,8,2304]{2,1,0:T(8,128)(2,1)} %bitcast.12), calls=%async_computation.2 | async-start | bytes 2359296 | tf_op jit(solution)/shard_map/all_to_all | solution.py:464
  133.5 6.0 %shard_map.160 = bf16[4,576,128]{2,1,0:T(8,128)(2,1)} custom-call(bf16[256,2304]{1,0:T(8,128)(2,1)S(1)} %copy-done.10, bf16[256,2304]{1,0:T(8,128)(2,1)S(1)} %copy-done.13, bf16[8,256,512]{2,1,0:T(8,128)(2,1)S(1)} %get-tuple-element.42.probs, bf16[512,512]{1,0:T(8,128)(2,1)S(1)} %copy-done.6, f32[1,512]{1,0:T(1,128)S(1)} %get-tuple-element.45.delta), custom_call_target="tpu_custom_call" | custom-call | flops 2281701376 | bytes 5572608 | tf_op jit(solution)/shard_map/pallas_call | solution.py:45
  139.5 8.8 %all-to-all-done.2 = bf16[32,8,2304]{2,1,0:T(8,128)(2,1)S(1)} async-done(((bf16[32,8,2304]{2,1,0:T(8,128)(2,1)}), bf16[32,8,2304]{2,1,0:T(8,128)(2,1)S(1)}, u32[]{:S(2)}, u32[]{:S(2)}) %all-to-all-start.2) | async-done | bytes 1179680 | tf_op jit(solution)/shard_map/all_to_all | solution.py:464
  152.8 1.9 %collective-permute-start.15 = (bf16[8,2304]{1,0:T(8,128)(2,1)S(1)}, bf16[8,2304]{1,0:T(8,128)(2,1)S(1)}, u32[]{:S(2)}, u32[]{:S(2)}) collective-permute-start(bf16[8,2304]{1,0:T(8,128)(2,1)S(1)} %shard_map.161.own), channel_id=1, source_target_pairs={{0,6},{2,0},{4,2},{6,4},{1,7},{3,1},{5,3},{7,5},{8,14},{10,8},{12,... | collective-permute-start | bytes 110600 | tf_op jit(solution)/shard_map/ppermute | solution.py:460
  154.7 2.5 %collective-permute-done.13.far = bf16[16,2304]{1,0:T(8,128)(2,1)S(1)} collective-permute-done((bf16[16,2304]{1,0:T(8,128)(2,1)S(1)}, bf16[16,2304]{1,0:T(8,128)(2,1)S(1)}, u32[]{:S(2)}, u32[]{:S(2)}) %collective-permute-start.13) | collective-permute-done | bytes 73760 | tf_op jit(solution)/shard_map/ppermute | solution.py:456
  157.2 2.9 %collective-permute-start.14 = (bf16[16,2304]{1,0:T(8,128)(2,1)S(1)}, bf16[16,2304]{1,0:T(8,128)(2,1)S(1)}, u32[]{:S(2)}, u32[]{:S(2)}) collective-permute-start(bf16[16,2304]{1,0:T(8,128)(2,1)S(1)} %collective-permute-done.13.far), channel_id=1, source_target_pairs={{0,1},{1,0},{2,3},{3,2},{4,5},{5,4},{6,7},{7,6},{8,9},{9,8},{10,11... | collective-permute-start | bytes 221192 | tf_op jit(solution)/shard_map/ppermute | solution.py:451
  (79 shorter events, 27.0 us)
Async XLA Ops:
  4.9 53.2 %copy-start.19 = (bf16[1,2304,512]{2,1,0:T(8,128)(2,1)S(1)}, bf16[1,2304,512]{2,1,0:T(8,128)(2,1)}, u32[]{:S(2)}) copy-start(bf16[1,2304,512]{2,1,0:T(8,128)(2,1)} %param.22) | copy-start | bytes 7077892
  4.9 53.2 %copy-start.20 = (bf16[1,2304,512]{2,1,0:T(8,128)(2,1)S(1)}, bf16[1,2304,512]{2,1,0:T(8,128)(2,1)}, u32[]{:S(2)}) copy-start(bf16[1,2304,512]{2,1,0:T(8,128)(2,1)} %param.23) | copy-start | bytes 7077892
  4.9 53.2 %copy-start.21 = (bf16[1,512,2304]{2,1,0:T(8,128)(2,1)S(1)}, bf16[1,512,2304]{2,1,0:T(8,128)(2,1)}, u32[]{:S(2)}) copy-start(bf16[1,512,2304]{2,1,0:T(8,128)(2,1)} %param.24) | copy-start | bytes 7077892
  62.6 21.4 %all-to-all-start.1 = ((bf16[32,8,2304]{2,1,0:T(8,128)(2,1)}), bf16[32,8,2304]{2,1,0:T(8,128)(2,1)S(1)}, u32[]{:S(2)}, u32[]{:S(2)}) async-start(bf16[32,8,2304]{2,1,0:T(8,128)(2,1)} %bitcast.8), calls=%async_computation.1 | async-start | bytes 2359296 | tf_op jit(solution)/shard_map/all_to_all | solution.py:464
  66.7 4.4 %collective-permute-start = (bf16[256,2304]{1,0:T(8,128)(2,1)S(1)}, bf16[256,2304]{1,0:T(8,128)(2,1)S(1)}, u32[]{:S(2)}, u32[]{:S(2)}) collective-permute-start(bf16[256,2304]{1,0:T(8,128)(2,1)S(1)} %get-tuple-element.28.mine_far.keys.mine), channel_id=1, source_target_pairs={{0,1},{1,0},{2,3},{3,2},{4,5},{5,4},{6,7},{7,6},{8,9},{9,8},{10,11... | collective-permute-start | bytes 3538952 | tf_op jit(solution)/shard_map/ppermute | solution.py:451
  84.0 33.3 %copy-start.15 = (f32[512,512]{1,0:T(8,128)S(1)}, f32[512,512]{1,0:T(8,128)}, u32[]{:S(2)}) copy-start(f32[512,512]{1,0:T(8,128)} %copy-done.14) | copy-start | bytes 3145732
  84.5 4.2 %collective-permute-start.1 = (bf16[64,2304]{1,0:T(8,128)(2,1)S(1)}, bf16[64,2304]{1,0:T(8,128)(2,1)S(1)}, u32[]{:S(2)}, u32[]{:S(2)}) collective-permute-start(bf16[64,2304]{1,0:T(8,128)(2,1)S(1)} %shard_map.153), channel_id=1, source_target_pairs={{0,1},{1,0},{2,3},{3,2},{4,5},{5,4},{6,7},{7,6},{8,9},{9,8},{10,11... | collective-permute-start | bytes 884744 | tf_op jit(solution)/shard_map/ppermute | solution.py:451
  87.6 29.7 %copy-start.16 = (bf16[4,512,128]{2,1,0:T(8,128)(2,1)S(1)}, bf16[4,512,128]{2,1,0:T(8,128)(2,1)}, u32[]{:S(2)}) copy-start(bf16[4,512,128]{2,1,0:T(8,128)(2,1)} %value_up.1) | copy-start | bytes 1572868
  88.8 11.2 %collective-permute-start.3 = (bf16[32,2304]{1,0:T(8,128)(2,1)S(1)}, bf16[32,2304]{1,0:T(8,128)(2,1)S(1)}, u32[]{:S(2)}, u32[]{:S(2)}) collective-permute-start(bf16[32,2304]{1,0:T(8,128)(2,1)S(1)} %get-tuple-element.36), channel_id=1, source_target_pairs={{0,4},{1,3},{2,6},{3,5},{4,0},{5,7},{6,2},{7,1},{8,12},{9,11},{10,... | collective-permute-start | bytes 442376 | tf_op jit(solution)/shard_map/ppermute | solution.py:456
  91.9 10.8 %collective-permute-start.5 = (bf16[16,2304]{1,0:T(8,128)(2,1)S(1)}, bf16[16,2304]{1,0:T(8,128)(2,1)S(1)}, u32[]{:S(2)}, u32[]{:S(2)}) collective-permute-start(bf16[16,2304]{1,0:T(8,128)(2,1)S(1)} %get-tuple-element.37), channel_id=1, source_target_pairs={{0,6},{2,0},{4,2},{6,4},{1,7},{3,1},{5,3},{7,5},{8,14},{10,8},{12,... | collective-permute-start | bytes 221192 | tf_op jit(solution)/shard_map/ppermute | solution.py:460
  100.0 4.1 %collective-permute-start.4 = (bf16[32,2304]{1,0:T(8,128)(2,1)S(1)}, bf16[32,2304]{1,0:T(8,128)(2,1)S(1)}, u32[]{:S(2)}, u32[]{:S(2)}) collective-permute-start(bf16[32,2304]{1,0:T(8,128)(2,1)S(1)} %collective-permute-done.3.far), channel_id=1, source_target_pairs={{0,1},{1,0},{2,3},{3,2},{4,5},{5,4},{6,7},{7,6},{8,9},{9,8},{10,11... | collective-permute-start | bytes 442376 | tf_op jit(solution)/shard_map/ppermute | solution.py:451
  101.3 1.9 %collective-permute-start.2 = (bf16[16,2304]{1,0:T(8,128)(2,1)S(1)}, bf16[16,2304]{1,0:T(8,128)(2,1)S(1)}, u32[]{:S(2)}, u32[]{:S(2)}) collective-permute-start(bf16[16,2304]{1,0:T(8,128)(2,1)S(1)} %get-tuple-element.35.own), channel_id=1, source_target_pairs={{0,1},{1,0},{2,3},{3,2},{4,5},{5,4},{6,7},{7,6},{8,9},{9,8},{10,11... | collective-permute-start | bytes 221192 | tf_op jit(solution)/shard_map/ppermute | solution.py:451
  102.7 1.4 collective-permute-start.6
  104.4 7.6 %collective-permute-start.7 = (bf16[32,2304]{1,0:T(8,128)(2,1)S(1)}, bf16[32,2304]{1,0:T(8,128)(2,1)S(1)}, u32[]{:S(2)}, u32[]{:S(2)}) collective-permute-start(bf16[32,2304]{1,0:T(8,128)(2,1)S(1)} %get-tuple-element.38.own), channel_id=1, source_target_pairs={{0,4},{1,3},{2,6},{3,5},{4,0},{5,7},{6,2},{7,1},{8,12},{9,11},{10,... | collective-permute-start | bytes 442376 | tf_op jit(solution)/shard_map/ppermute | solution.py:456
  106.0 10.0 %collective-permute-start.9 = (bf16[16,2304]{1,0:T(8,128)(2,1)S(1)}, bf16[16,2304]{1,0:T(8,128)(2,1)S(1)}, u32[]{:S(2)}, u32[]{:S(2)}) collective-permute-start(bf16[16,2304]{1,0:T(8,128)(2,1)S(1)} %get-tuple-element.39), channel_id=1, source_target_pairs={{0,6},{2,0},{4,2},{6,4},{1,7},{3,1},{5,3},{7,5},{8,14},{10,8},{12,... | collective-permute-start | bytes 221192 | tf_op jit(solution)/shard_map/ppermute | solution.py:460
  112.0 5.3 %collective-permute-start.8 = (bf16[32,2304]{1,0:T(8,128)(2,1)S(1)}, bf16[32,2304]{1,0:T(8,128)(2,1)S(1)}, u32[]{:S(2)}, u32[]{:S(2)}) collective-permute-start(bf16[32,2304]{1,0:T(8,128)(2,1)S(1)} %collective-permute-done.7.far), channel_id=1, source_target_pairs={{0,1},{1,0},{2,3},{3,2},{4,5},{5,4},{6,7},{7,6},{8,9},{9,8},{10,11... | collective-permute-start | bytes 442376 | tf_op jit(solution)/shard_map/ppermute | solution.py:451
  116.0 1.3 collective-permute-start.10
  121.6 2.9 %collective-permute-start.11 = (bf16[256,2304]{1,0:T(8,128)(2,1)S(1)}, bf16[256,2304]{1,0:T(8,128)(2,1)S(1)}, u32[]{:S(2)}, u32[]{:S(2)}) collective-permute-start(bf16[256,2304]{1,0:T(8,128)(2,1)S(1)} %shard_map.158), channel_id=1, source_target_pairs={{0,1},{1,0},{2,3},{3,2},{4,5},{5,4},{6,7},{7,6},{8,9},{9,8},{10,11... | collective-permute-start | bytes 3538952 | tf_op jit(solution)/shard_map/ppermute | solution.py:451
  125.7 22.5 %all-to-all-start.2 = ((bf16[32,8,2304]{2,1,0:T(8,128)(2,1)}), bf16[32,8,2304]{2,1,0:T(8,128)(2,1)S(1)}, u32[]{:S(2)}, u32[]{:S(2)}) async-start(bf16[32,8,2304]{2,1,0:T(8,128)(2,1)} %bitcast.12), calls=%async_computation.2 | async-start | bytes 2359296 | tf_op jit(solution)/shard_map/all_to_all | solution.py:464
  148.4 2.6 %collective-permute-start.12 = (bf16[8,2304]{1,0:T(8,128)(2,1)S(1)}, bf16[8,2304]{1,0:T(8,128)(2,1)S(1)}, u32[]{:S(2)}, u32[]{:S(2)}) collective-permute-start(bf16[8,2304]{1,0:T(8,128)(2,1)S(1)} %shard_map.161.own), channel_id=1, source_target_pairs={{0,1},{1,0},{2,3},{3,2},{4,5},{5,4},{6,7},{7,6},{8,9},{9,8},{10,11... | collective-permute-start | bytes 110600 | tf_op jit(solution)/shard_map/ppermute | solution.py:451
  151.0 6.2 %collective-permute-start.13 = (bf16[16,2304]{1,0:T(8,128)(2,1)S(1)}, bf16[16,2304]{1,0:T(8,128)(2,1)S(1)}, u32[]{:S(2)}, u32[]{:S(2)}) collective-permute-start(bf16[16,2304]{1,0:T(8,128)(2,1)S(1)} %shard_map.162.own), channel_id=1, source_target_pairs={{0,4},{1,3},{2,6},{3,5},{4,0},{5,7},{6,2},{7,1},{8,12},{9,11},{10,... | collective-permute-start | bytes 221192 | tf_op jit(solution)/shard_map/ppermute | solution.py:456
  152.8 7.3 %collective-permute-start.15 = (bf16[8,2304]{1,0:T(8,128)(2,1)S(1)}, bf16[8,2304]{1,0:T(8,128)(2,1)S(1)}, u32[]{:S(2)}, u32[]{:S(2)}) collective-permute-start(bf16[8,2304]{1,0:T(8,128)(2,1)S(1)} %shard_map.161.own), channel_id=1, source_target_pairs={{0,6},{2,0},{4,2},{6,4},{1,7},{3,1},{5,3},{7,5},{8,14},{10,8},{12,... | collective-permute-start | bytes 110600 | tf_op jit(solution)/shard_map/ppermute | solution.py:460
  157.2 4.6 %collective-permute-start.14 = (bf16[16,2304]{1,0:T(8,128)(2,1)S(1)}, bf16[16,2304]{1,0:T(8,128)(2,1)S(1)}, u32[]{:S(2)}, u32[]{:S(2)}) collective-permute-start(bf16[16,2304]{1,0:T(8,128)(2,1)S(1)} %collective-permute-done.13.far), channel_id=1, source_target_pairs={{0,1},{1,0},{2,3},{3,2},{4,5},{5,4},{6,7},{7,6},{8,9},{9,8},{10,11... | collective-permute-start | bytes 221192 | tf_op jit(solution)/shard_map/ppermute | solution.py:451
  160.1 1.7 %collective-permute-start.16 = (bf16[8,2304]{1,0:T(8,128)(2,1)S(1)}, bf16[8,2304]{1,0:T(8,128)(2,1)S(1)}, u32[]{:S(2)}, u32[]{:S(2)}) collective-permute-start(bf16[8,2304]{1,0:T(8,128)(2,1)S(1)} %collective-permute-done.15.near), channel_id=1, source_target_pairs={{0,1},{1,0},{2,3},{3,2},{4,5},{5,4},{6,7},{7,6},{8,9},{9,8},{10,11... | collective-permute-start | bytes 110600 | tf_op jit(solution)/shard_map/ppermute | solution.py:451
  (19 other events, 147.3 us)
